TPU v7x, 1024 devices: a whole 4x8x16 slice. The times are simulated.
1024 devices in a mesh: row: 32 (over x_hi, z), col: 32 (over x_lo, y, core).
Axes of the slice: x: 4 (x_hi: 2, x_lo: 2; x = x_hi * 2 + x_lo), y: 8, z: 16, core: 2. Of those that a mesh axis runs over, the one named last changes fastest.
Arguments:
- inputs: bfloat16 [128, 12288], P('col', 'row'), may hold values from -6 to 6
- weight_in: bfloat16 [12288, 24576], P('row', 'col'), may hold values from -0.0546875 to 0.0546875
- weight_out: bfloat16 [24576, 12288], P('col', 'row'), may hold values from -0.0390625 to 0.0390625
- grad_out: bfloat16 [128, 12288], P('col', 'row'), may hold values from -0.8984375 to 0.8984375
Outputs:
- block_out: bfloat16 [128, 12288], P('col', 'row')
- grad_inputs: bfloat16 [128, 12288], P('col', 'row')
- grad_weight_in: bfloat16 [12288, 24576], P('row', 'col')
- grad_weight_out: bfloat16 [24576, 12288], P('col', 'row')
All inputs are finite; a program needn't handle non-finite values.
Results may differ from a plain program's by a relative error of at most 0.0061.
Values may be sent and summed in bfloat16 or wider, within the bound.
A program may use at most 32 MiB of HBM per device.

v0:
```python
import math

import jax
import jax.numpy as jnp
from jax import lax
from jax.sharding import PartitionSpec as P

gelu_coef = math.sqrt(2.0 / math.pi)


def gelu_value(value):
    inner = gelu_coef * (value + 0.044715 * value * value * value)
    return 0.5 * value * (1.0 + jnp.tanh(inner))


def gelu_slope(value):
    inner = gelu_coef * (value + 0.044715 * value * value * value)
    tanh_value = jnp.tanh(inner)
    return 0.5 * (1.0 + tanh_value) + 0.5 * value * (1.0 - tanh_value * tanh_value) * gelu_coef * (
        1.0 + 3.0 * 0.044715 * value * value
    )


def sum_rows(maker, rows):
    return lax.psum_scatter(
        maker(jnp.int32(0), rows * lax.axis_size("row")), "row", scatter_dimension=0, tiled=True
    )


def sum_cols(maker, rows):
    return lax.psum_scatter(
        maker(jnp.int32(0), rows * lax.axis_size("col")), "col", scatter_dimension=0, tiled=True
    )


def hidden_all(local_part):
    return lax.all_gather(local_part, "row", axis=0, tiled=True)


def contract_last(left, right):
    return lax.dot_general(
        left, right, (((1,), (1,)), ((), ())), preferred_element_type=jnp.float32
    )


def contract_first(left, right):
    return lax.dot_general(
        left, right, (((0,), (0,)), ((), ())), preferred_element_type=jnp.float32
    )


def local(inputs, weight_in, weight_out, grad_out):
    inputs_all, grad_all = (
        lax.all_gather(inputs, "col", axis=0, tiled=True),
        lax.all_gather(grad_out, "col", axis=0, tiled=True),
    )
    total = inputs_all.shape[0]
    row_share = total // lax.axis_size("row")
    col_share = total // lax.axis_size("col")

    def pre_term(start, count):
        return jnp.dot(inputs_all, weight_in, preferred_element_type=jnp.float32)

    pre_local = sum_rows(pre_term, row_share).astype(jnp.bfloat16)
    pre_gelu = hidden_all(pre_local)
    pre_float = pre_gelu.astype(jnp.float32)
    activation = gelu_value(pre_float).astype(jnp.bfloat16)

    def out_term(start, count):
        return jnp.dot(activation, weight_out, preferred_element_type=jnp.float32)

    block_out = sum_cols(out_term, col_share).astype(jnp.bfloat16)
    grad_weight_out = contract_first(activation, grad_all).astype(jnp.bfloat16)

    def grad_term(start, count):
        return contract_last(grad_all, weight_out)

    grad_activation = sum_rows(grad_term, row_share)
    grad_pre_local = (grad_activation * gelu_slope(pre_local.astype(jnp.float32))).astype(
        jnp.bfloat16
    )
    grad_pre_gelu = hidden_all(grad_pre_local)
    grad_weight_in = contract_first(inputs_all, grad_pre_gelu).astype(jnp.bfloat16)

    def input_term(start, count):
        return contract_last(grad_pre_gelu, weight_in)

    grad_inputs = sum_cols(input_term, col_share).astype(jnp.bfloat16)
    return (block_out, grad_inputs, grad_weight_in, grad_weight_out)


def solution(mesh):
    placed = (P("col", "row"), P("row", "col"), P("col", "row"), P("col", "row"))
    return jax.shard_map(
        local,
        mesh=mesh,
        in_specs=placed,
        out_specs=(P("col", "row"), P("col", "row"), P("row", "col"), P("col", "row")),
        check_vma=False,
    )
```

profile of v0, /device:TPU:1, one launch (start us, length us, event | category | flops | bytes accessed | tf_op | source)
XLA Modules:
  0.0 529.5 jit_solution(1404844700108990214)
XLA Ops:
  7.2 0.0 copy-start
  7.2 0.0 all-reduce.9.cloned.1.call-start
  7.2 45.1 %all-gather.2 = bf16[32,4,384]{2,1,0:T(4,128)(2,1)S(1)} all-gather(bf16[1,4,384]{2,1,0:T(4,128)(2,1)} %bitcast.20), channel_id=1, replica_groups=mesh['row'=32,'col'=32] {'col'}, dimensions={0}, use_global_device_ids=true | all-gather | bytes 101376 | tf_op jit(solution)/shard_map/all_gather | solution.py:55
  52.3 0.0 copy-done
  52.3 0.0 copy-start.2
  52.3 1.1 fusion.21
  53.4 0.0 copy-start.1
  53.4 0.0 all-reduce.9.cloned.1.call-update
  53.4 0.0 copy-done.2
  53.5 32.7 %all-gather = bf16[32,4,384]{2,1,0:T(4,128)(2,1)S(1)} all-gather(bf16[1,4,384]{2,1,0:T(4,128)(2,1)S(1)} %bitcast.21), channel_id=1, replica_groups=mesh['row'=32,'col'=32] {'col'}, dimensions={0}, use_global_device_ids=true | all-gather | bytes 101376 | tf_op jit(solution)/shard_map/all_gather | solution.py:54
  86.1 0.0 copy-done.1
  86.2 0.3 fusion.20
  86.4 129.7 %all-reduce.10 = bf16[128,768]{1,0:T(8,128)(2,1)S(1)} all-reduce(f32[128,768]{1,0:T(8,128)S(1)} %fusion.20), channel_id=2, replica_groups=mesh['row'=32,'col'=32] {'row'}, use_global_device_ids=true, to_apply=%region_0.0.clone | all-reduce | flops 98304 | bytes 589824
  216.1 1.3 dynamic-slice
  218.1 59.7 %all-gather.1 = bf16[32,4,768]{2,1,0:T(4,128)(2,1)S(1)} all-gather(bf16[1,4,768]{2,1,0:T(4,128)(2,1)S(1)} %fusion.16), channel_id=1, replica_groups=mesh['row'=32,'col'=32] {'row'}, dimensions={0}, use_global_device_ids=true | all-gather | bytes 202752 | tf_op jit(solution)/shard_map/all_gather | solution.py:37
  277.8 0.3 fusion.18
  278.1 1.3 dynamic-slice.2
  280.0 1.2 convolution_convert_fusion
  281.2 40.7 %all-reduce.9.cloned.1.call-done = f32[128,768]{1,0:T(8,128)} async-done(((f32[128,768]{1,0:T(8,128)}), f32[128,768]{1,0:T(8,128)}) %all-reduce.9.cloned.1.call-update) | async-done | bytes 393232
  321.9 0.8 fusion.15
  322.7 62.5 %all-gather.3 = bf16[32,4,768]{2,1,0:T(4,128)(2,1)S(1)} all-gather(bf16[1,4,768]{2,1,0:T(4,128)(2,1)S(1)} %fusion.15), channel_id=1, replica_groups=mesh['row'=32,'col'=32] {'row'}, dimensions={0}, use_global_device_ids=true | all-gather | bytes 202752 | tf_op jit(solution)/shard_map/all_gather | solution.py:37
  385.2 0.1 reshape.15
  385.2 0.3 fusion.22
  385.5 0.3 fusion
  385.9 1.1 copy.9
  387.0 135.0 %all-reduce.11 = (bf16[128,384]{1,0:T(8,128)(2,1)S(1)}, bf16[128,384]{1,0:T(8,128)(2,1)S(1)}) all-reduce(f32[128,384]{1,0:T(8,128)S(1)} %fusion.18, f32[128,384]{1,0:T(8,128)S(1)} %fusion.22), channel_id=3, replica_groups=mesh['row'=32,'col'=32] {'col'}, use_global_device_ids=true, to_apply=%region_1.0.clone | all-reduce | flops 98304 | bytes 589824
  522.0 0.6 dynamic-slice_convert_fusion.1
  (4 shorter events, 0.1 us)
Async XLA Ops:
  7.2 45.2 %copy-start = (bf16[768,384]{1,0:T(8,128)(2,1)S(1)}, bf16[768,384]{1,0:T(8,128)(2,1)}, u32[]{:S(2)}) copy-start(bf16[768,384]{1,0:T(8,128)(2,1)} %param.6) | copy-start | bytes 1769476
  7.2 314.7 %all-reduce.9.cloned.1.call-start = ((), (), s32[]{:S(2)}) async-start(), calls=%async_computation | async-start | bytes 786432
  52.3 1.1 copy-start.2
  53.4 32.7 %copy-start.1 = (bf16[384,768]{1,0:T(8,128)(2,1)S(1)}, bf16[384,768]{1,0:T(8,128)(2,1)}, u32[]{:S(2)}) copy-start(bf16[384,768]{1,0:T(8,128)(2,1)} %param.5) | copy-start | bytes 1769476
Sparse Core Ops, SparseCore 0:
  53.6 268.3 all-reduce.8
where the time goes:
time: 533 us; the launch traced here: 529 us
  blocking collectives  465 us (87%)
  waiting for transfers between devices  40.7 us (8%)
  between operations  15.4 us (3%)
    unnamed x2, blocking collectives  265 us
    all_gather x2, blocking collectives, hidden_all(): return lax.all_gather(local_part, 'row', axis=0, tiled=True)  122 us
    all_gather x1, blocking collectives, local(): lax.all_gather(grad_out, 'col', axis=0, tiled=True)  45.1 us
    unnamed x2, waiting for transfers between devices  40.7 us
    all_gather x1, blocking collectives, local(): lax.all_gather(inputs, 'col', axis=0, tiled=True)  32.7 us
  transfers between devices with their start and end apart: 1, of which 1 were waited for; matrix products, arithmetic and copies ran while one was open for 1% of the time, Pallas kernels for 0%

commit v1 on v0

v1 whole, which is shorter than its diff:
```python
import functools
import math

import jax
import jax.numpy as jnp
from jax import lax
from jax.experimental import pallas as pl
from jax.experimental.pallas import tpu as pltpu
from jax.sharding import PartitionSpec as P

MESH = pl.DeviceIdType.MESH
F32, BF16 = jnp.float32, jnp.bfloat16
gelu_coef = math.sqrt(2.0 / math.pi)
Z, Y = 16, 8

row_offsets = sorted(
    [(h, k) for h in range(2) for k in range(Z) if (h, k) != (0, 0)],
    key=lambda t: -(min(t[1], Z - t[1]) + 2 * t[0]),
)
chip_offsets = sorted(
    [(h, k) for h in range(2) for k in range(Y) if (h, k) != (0, 0)],
    key=lambda t: -(min(t[1], Y - t[1]) + t[0]),
)
n_row, n_chip = len(row_offsets), len(chip_offsets)


def gelu_value(value):
    inner = gelu_coef * (value + 0.044715 * value * value * value)
    return 0.5 * value * (1.0 + jnp.tanh(inner))


def gelu_slope(value):
    inner = gelu_coef * (value + 0.044715 * value * value * value)
    tanh_value = jnp.tanh(inner)
    return 0.5 * (1.0 + tanh_value) + 0.5 * value * (1.0 - tanh_value * tanh_value) * gelu_coef * (
        1.0 + 3.0 * 0.044715 * value * value
    )


def dot(left, right, left_dim, right_dim):
    return lax.dot_general(
        left, right, (((left_dim,), (right_dim,)), ((), ())), preferred_element_type=F32
    )


def pack(value):
    first, second, third = value[..., :128], value[..., 128:256], value[..., 256:]
    return jnp.concatenate(
        [jnp.concatenate([first, second], axis=-2), jnp.concatenate([third, third], axis=-2)], axis=-1
    ).astype(BF16)


def unpack(value):
    wide = value.astype(F32)
    return jnp.concatenate([wide[..., :8, :128], wide[..., 8:, :128], wide[..., :8, 128:]], axis=-1)


def kernel(
    inputs_ref, weight_in_ref, weight_out_ref, grad_ref,
    out_ref, grad_inputs_ref, grad_weight_in_ref, grad_weight_out_ref,
    eight, mine, gathered, swapped, sums, parts, hidden, product, pair_out, pair_in, chip_out, chip_in,
    send1, recv1, send_core1, recv_core1, send2, recv2, send3, recv3, send_core4, recv_core4, send4, recv4,
):
    row, col = lax.axis_index("row"), lax.axis_index("col")
    x_hi, z = row // Z, row % Z
    chip, core = col // 2, col % 2
    x_lo, y = chip // Y, chip % Y
    partner = (row, chip * 2 + 1 - core)

    def row_peer(offset, sign=1):
        return (x_hi + offset[0]) % 2, (z + sign * offset[1] + Z) % Z

    def chip_peer(offset, sign=1):
        return ((x_lo + offset[0]) % 2) * Y + (y + sign * offset[1] + Y) % Y

    barrier = pltpu.get_barrier_semaphore()
    for offset in chip_offsets:
        pl.semaphore_signal(barrier, inc=1, device_id=(row, chip_peer(offset) * 2 + core), device_id_type=MESH)
    for offset in row_offsets:
        to_x, to_z = row_peer(offset)
        pl.semaphore_signal(barrier, inc=1, device_id=(to_x * Z + to_z, col), device_id_type=MESH)
    pl.semaphore_signal(barrier, inc=1, device_id=partner, device_id_type=MESH)

    def remote(src, dst, send, recv, device):
        return pltpu.make_async_remote_copy(
            src_ref=src, dst_ref=dst, send_sem=send, recv_sem=recv, device_id=device, device_id_type=MESH
        )

    started = []

    def go(*args):
        copy = remote(*args)
        copy.start()
        started.append(copy)

    eight[0:4, :] = inputs_ref[...].astype(F32)
    eight[4:8, :] = grad_ref[...].astype(F32)
    mine[...] = pack(eight[...])
    gathered[col] = mine[...]
    pl.semaphore_wait(barrier, n_row + n_chip + 1)
    for i, offset in enumerate(chip_offsets):
        go(mine, gathered.at[col], send1.at[i], recv1.at[i], (row, chip_peer(offset) * 2 + core))
    go(mine, gathered.at[col], send_core1.at[n_chip], recv_core1.at[n_chip], partner)
    for i in reversed(range(n_chip)):
        source = chip_peer(chip_offsets[i], -1) * 2
        here = gathered.at[source + core]
        remote(mine, here, send1.at[i], recv1.at[i], partner).wait_recv()
        go(here, here, send_core1.at[i], recv_core1.at[i], partner)
    for i in reversed(range(n_chip)):
        source = chip_peer(chip_offsets[i], -1) * 2
        remote(mine, gathered.at[source + 1 - core], send_core1.at[i], recv_core1.at[i], partner).wait_recv()
    remote(mine, gathered.at[partner[1]], send_core1.at[n_chip], recv_core1.at[n_chip], partner).wait_recv()

    groups = unpack(gathered[...])
    swapped[...] = pltpu.roll(groups, 4, 1).reshape(256, 384).astype(BF16)
    stacked = groups.reshape(256, 384).astype(BF16)

    def upper(width):
        return lax.broadcasted_iota(jnp.int32, (256, width), 0) % 8 < 4

    for half in range(2):
        cut = slice(half * 384, half * 384 + 384)
        first = dot(stacked, weight_in_ref[:, cut], 1, 0)
        second = dot(stacked, weight_out_ref[cut, :], 1, 1)
        sums[half] = jnp.where(upper(384), first, second).astype(BF16).reshape(Z, 16, 384)
    for i, offset in enumerate(row_offsets):
        to_x, to_z = row_peer(offset)
        go(sums.at[to_x, to_z], parts.at[i], send2.at[i], recv2.at[i], (to_x * Z + to_z, col))
    total = sums[x_hi, z].astype(F32)
    for i in reversed(range(n_row)):
        remote(sums.at[x_hi, z], parts.at[i], send2.at[i], recv2.at[i], partner).wait_recv()
        total += parts[i].astype(F32)

    total = total.reshape(2, 8, 384)
    pre = pltpu.roll(total, 4, 1).astype(BF16).astype(F32)
    own = total.astype(BF16).astype(F32)
    act_row = lax.broadcasted_iota(jnp.int32, (2, 8, 384), 1) < 4
    hidden[x_hi, z] = jnp.where(act_row, gelu_value(own), total * gelu_slope(pre)).astype(BF16).reshape(16, 384)
    for i, offset in enumerate(row_offsets):
        to_x, to_z = row_peer(offset)
        go(hidden.at[x_hi, z], hidden.at[x_hi, z], send3.at[i], recv3.at[i], (to_x * Z + to_z, col))
    for i in reversed(range(n_row)):
        from_x, from_z = row_peer(row_offsets[i], -1)
        here = hidden.at[from_x, from_z]
        remote(here, here, send3.at[i], recv3.at[i], partner).wait_recv()

    halves = [hidden[half].reshape(256, 384) for half in range(2)]
    first = dot(halves[0], weight_out_ref[:384, :], 1, 0) + dot(halves[1], weight_out_ref[384:, :], 1, 0)
    second = dot(halves[0], weight_in_ref[:, :384], 1, 1) + dot(halves[1], weight_in_ref[:, 384:], 1, 1)
    product[...] = jnp.where(upper(384), first, second).reshape(16, 2, 8, 384)
    pair_out[...] = pack(product[:, pl.ds(1 - core, 1)].reshape(16, 8, 384))
    go(pair_out, pair_in, send_core4, recv_core4, partner)
    remote(pair_out, pair_in, send_core4, recv_core4, partner).wait_recv()
    both = product[:, pl.ds(core, 1)].reshape(16, 8, 384) + unpack(pair_in[...])
    chip_out[...] = pack(both)
    for i, offset in enumerate(chip_offsets):
        to = chip_peer(offset)
        go(chip_out.at[to], chip_in.at[i], send4.at[i], recv4.at[i], (row, to * 2 + core))

    for half in range(2):
        cut = slice(half * 384, half * 384 + 384)
        here = halves[half]
        act = jnp.where(upper(384), here.astype(F32), 0.0).astype(BF16)
        grad_pre = jnp.where(upper(384), 0.0, here.astype(F32)).astype(BF16)
        grad_weight_out_ref[cut, :] = dot(act, swapped[...], 0, 0).astype(BF16)
        grad_weight_in_ref[:, cut] = dot(swapped[...], grad_pre, 0, 0).astype(BF16)

    result = unpack(chip_out[chip])
    for i in reversed(range(n_chip)):
        remote(chip_out.at[chip], chip_in.at[i], send4.at[i], recv4.at[i], partner).wait_recv()
        result += unpack(chip_in[i])
    eight[...] = result
    out_ref[...] = eight[0:4, :].astype(BF16)
    grad_inputs_ref[...] = eight[4:8, :].astype(BF16)
    for copy in started:
        copy.wait_send()


def local(inputs, weight_in, weight_out, grad_out):
    vmem = pl.BlockSpec(memory_space=pltpu.VMEM)
    dma = pltpu.SemaphoreType.DMA
    return pl.pallas_call(
        kernel,
        out_shape=(
            jax.ShapeDtypeStruct(inputs.shape, BF16),
            jax.ShapeDtypeStruct(inputs.shape, BF16),
            jax.ShapeDtypeStruct(weight_in.shape, BF16),
            jax.ShapeDtypeStruct(weight_out.shape, BF16),
        ),
        in_specs=[vmem] * 4,
        out_specs=[vmem] * 4,
        scratch_shapes=[
            pltpu.VMEM((8, 384), F32),
            pltpu.VMEM((16, 256), BF16),
            pltpu.VMEM((32, 16, 256), BF16),
            pltpu.VMEM((256, 384), BF16),
            pltpu.VMEM((2, Z, 16, 384), BF16),
            pltpu.VMEM((n_row, 16, 384), BF16),
            pltpu.VMEM((2, Z, 16, 384), BF16),
            pltpu.VMEM((16, 2, 8, 384), F32),
            pltpu.VMEM((16, 16, 256), BF16),
            pltpu.VMEM((16, 16, 256), BF16),
            pltpu.VMEM((16, 16, 256), BF16),
            pltpu.VMEM((n_chip, 16, 256), BF16),
            dma((n_chip,)), dma((n_chip,)), dma((n_chip + 1,)), dma((n_chip + 1,)),
            dma((n_row,)), dma((n_row,)), dma((n_row,)), dma((n_row,)),
            dma, dma, dma((n_chip,)), dma((n_chip,)),
        ],
        compiler_params=pltpu.CompilerParams(
            collective_id=0, has_side_effects=True, vmem_limit_bytes=32 * 2**20
        ),
    )(inputs, weight_in, weight_out, grad_out)


def solution(mesh):
    placed = (P("col", "row"), P("row", "col"), P("col", "row"), P("col", "row"))
    return jax.shard_map(
        local,
        mesh=mesh,
        in_specs=placed,
        out_specs=(P("col", "row"), P("col", "row"), P("row", "col"), P("col", "row")),
        check_vma=False,
    )
```

time: 533 us -> 87.5 us (0.16)
  blocking collectives: 465 us -> 0 us
  Pallas kernels: 0 us -> 80.3 us
  waiting for transfers between devices: 40.7 us -> 0 us
  between operations: 15.4 us -> 0.65 us
    unnamed x2 -> x0, blocking collectives: 265 us -> none
    all_gather x4 -> x0, blocking collectives: 200 us -> none  [the longest x2 122 us: hidden_all(): return lax.all_gather(local_part, 'row', axis=0, tiled=True)]
    pallas_call x0 -> x1, Pallas kernels: none -> 80.3 us  [local(): pl.pallas_call(kernel, out_shape=(jax.ShapeDtypeStruct(inputs.shape, BF16...]
    unnamed x2 -> x0, waiting for transfers between devices: 40.7 us -> none
  transfers between devices with their start and end apart: 1 -> 0, of which waited for: 1 -> 0; matrix products, arithmetic and copies ran while one was open for 1% -> 0% of each run, Pallas kernels for 0% -> 0%
where the time goes in v1:
time: 87.5 us; the launch traced here: 87.2 us
  Pallas kernels  80.3 us (92%)
  local copies, waits for them, and re-layouts  6.27 us (7%)
    pallas_call x1, Pallas kernels, local(): pl.pallas_call(kernel, out_shape=(jax.ShapeDtypeStruct(inputs.shape, BF16...  80.3 us
    unnamed x12, local copies, waits for them, and re-layouts  6.27 us

profile of v1, /device:TPU:1, one launch (start us, length us, event | category | flops | bytes accessed | tf_op | source)
XLA Modules:
  0.0 87.2 jit_solution(10145829425269398106)
XLA Ops:
  0.6 0.0 copy-start
  0.6 1.1 %copy-done = bf16[384,768]{1,0:T(8,128)(2,1)S(1)} copy-done((bf16[384,768]{1,0:T(8,128)(2,1)S(1)}, bf16[384,768]{1,0:T(8,128)(2,1)}, u32[]{:S(2)}) %copy-start) | copy-done | bytes 589848
  1.7 0.0 copy-start.1
  1.7 1.1 %copy-done.1 = bf16[768,384]{1,0:T(8,128)(2,1)S(1)} copy-done((bf16[768,384]{1,0:T(8,128)(2,1)S(1)}, bf16[768,384]{1,0:T(8,128)(2,1)}, u32[]{:S(2)}) %copy-start.1) | copy-done | bytes 589848
  2.8 0.0 copy-start.2
  2.8 0.7 copy-done.2
  3.4 0.0 copy-start.3
  3.4 0.7 copy-done.3
  4.1 80.3 %shard_map.75 = (bf16[4,384]{1,0:T(4,128)(2,1)S(1)}, bf16[4,384]{1,0:T(4,128)(2,1)S(1)}, bf16[384,768]{1,0:T(8,128)(2,1)S(1)}, bf16[768,384]{1,0:T(8,128)(2,1)S(1)}) custom-call(bf16[4,384]{1,0:T(4,128)(2,1)S(1)} %copy-done.2, bf16[384,768]{1,0:T(8,128)(2,1)S(1)} %copy-done, bf16[768,384]{1,0:T(8,128)(2,1)S(1)} %copy-done.1, bf16[4,384]{1,0:T(4,128)(2,1)S(1)} %copy-done.3), custom_call_target="tpu_custom_call" | custom-call | tf_op jit(solution)/shard_map/pallas_call | solution.py:182
  84.4 0.6 copy.12
  85.0 0.6 copy.13
  85.6 0.8 copy.14
  86.4 0.8 copy.15
Async XLA Ops:
  0.6 1.1 %copy-start = (bf16[384,768]{1,0:T(8,128)(2,1)S(1)}, bf16[384,768]{1,0:T(8,128)(2,1)}, u32[]{:S(2)}) copy-start(bf16[384,768]{1,0:T(8,128)(2,1)} %weight_in_ref.1) | copy-start | bytes 1769476
  1.7 1.1 %copy-start.1 = (bf16[768,384]{1,0:T(8,128)(2,1)S(1)}, bf16[768,384]{1,0:T(8,128)(2,1)}, u32[]{:S(2)}) copy-start(bf16[768,384]{1,0:T(8,128)(2,1)} %weight_out_ref.1) | copy-start | bytes 1769476
  2.8 0.7 copy-start.2
  3.4 0.7 copy-start.3

commit v2 on v1

v2 whole, which is shorter than its diff:
```python
import functools
import math

import jax
import jax.numpy as jnp
from jax import lax
from jax.experimental import pallas as pl
from jax.experimental.pallas import tpu as pltpu
from jax.sharding import PartitionSpec as P

MESH = pl.DeviceIdType.MESH
F32, BF16 = jnp.float32, jnp.bfloat16
gelu_coef = math.sqrt(2.0 / math.pi)
Z, Y = 16, 8

cuts = ((0, 256), (256, 128))
n_cut = len(cuts)


def far_offsets(near):
    return [Z // 2] + [k for d in range(Z // 2 - 1, near, -1) for k in (d, Z - d)]


def near_offsets(near):
    return [k for d in range(near, 0, -1) for k in (d, Z - d)]


near_sum, near_send = 2, 2
chip_offsets = sorted(
    [(h, k) for h in range(2) for k in range(Y) if (h, k) != (0, 0)],
    key=lambda t: -(min(t[1], Y - t[1]) + t[0]),
)
n_chip = len(chip_offsets)
n_row = 31


def gelu_value(value):
    inner = gelu_coef * (value + 0.044715 * value * value * value)
    return 0.5 * value * (1.0 + jnp.tanh(inner))


def gelu_slope(value):
    inner = gelu_coef * (value + 0.044715 * value * value * value)
    tanh_value = jnp.tanh(inner)
    return 0.5 * (1.0 + tanh_value) + 0.5 * value * (1.0 - tanh_value * tanh_value) * gelu_coef * (
        1.0 + 3.0 * 0.044715 * value * value
    )


def dot(left, right, left_dim, right_dim):
    return lax.dot_general(
        left, right, (((left_dim,), (right_dim,)), ((), ())), preferred_element_type=F32
    )


def pack(value):
    first, second, third = value[..., :128], value[..., 128:256], value[..., 256:]
    return jnp.concatenate(
        [jnp.concatenate([first, second], axis=-2), jnp.concatenate([third, third], axis=-2)], axis=-1
    ).astype(BF16)


def unpack(value):
    wide = value.astype(F32)
    return jnp.concatenate([wide[..., :8, :128], wide[..., 8:, :128], wide[..., :8, 128:]], axis=-1)


def mix(first, second):
    low = lax.broadcasted_iota(jnp.int32, first.shape, 1) < 4
    return (
        jnp.where(low, first, pltpu.roll(second, 4, 1)),
        jnp.where(low, pltpu.roll(first, 4, 1), second),
    )


def kernel(
    inputs_hbm, weight_in_hbm, weight_out_hbm, grad_hbm,
    out_hbm, grad_inputs_hbm, grad_weight_in_hbm, grad_weight_out_hbm,
    out_ref, grad_inputs_ref, grad_weight_in_ref, grad_weight_out_ref,
    inputs_ref, weight_in_ref, weight_out_ref, grad_ref,
    eight, mine, gathered, tokens, spread, product, pair_in, chip_out, chip_in, *rest,
):
    per_cut = [rest[6 * p : 6 * p + 6] for p in range(n_cut)]
    (
        fetch, keep, entered, send1, recv1, send_core1, recv_core1, send_x2, recv_x2, send2, recv2,
        send3, recv3, send_x3, recv_x3, send_core4, recv_core4, send4, recv4,
    ) = rest[6 * n_cut :]
    row, col = lax.axis_index("row"), lax.axis_index("col")
    x_hi, z = row // Z, row % Z
    chip, core = col // 2, col % 2
    x_lo, y = chip // Y, chip % Y
    partner = (row, chip * 2 + 1 - core)
    opposite = ((1 - x_hi) * Z + z, col)

    def at_z(offset):
        return (z + offset) % Z

    def own_plane(offset):
        return (x_hi * Z + at_z(offset), col)

    def other_plane(offset):
        return ((1 - x_hi) * Z + at_z(offset), col)

    def chip_peer(offset, sign=1):
        return ((x_lo + offset[0]) % 2) * Y + (y + sign * offset[1] + Y) % Y

    def greet(semaphore, device):
        pl.semaphore_signal(semaphore, inc=1, device_id=device, device_id_type=MESH)

    barrier = pltpu.get_barrier_semaphore()
    for offset in chip_offsets:
        greet(barrier, (row, chip_peer(offset) * 2 + core))
    near_own, near_other = near_offsets(4), near_offsets(max(near_sum, near_send)) + [0]
    for offset in near_own:
        greet(barrier, own_plane(offset))
    for offset in near_other:
        greet(barrier, other_plane(offset))
    greet(barrier, partner)

    fetches = [
        pltpu.make_async_copy(src, dst, fetch.at[i])
        for i, (src, dst) in enumerate((
            (inputs_hbm, inputs_ref), (grad_hbm, grad_ref), (weight_in_hbm, weight_in_ref), (weight_out_hbm, weight_out_ref),
        ))
    ]
    for copy in fetches:
        copy.start()

    def remote(src, dst, send, recv, device):
        return pltpu.make_async_remote_copy(
            src_ref=src, dst_ref=dst, send_sem=send, recv_sem=recv, device_id=device, device_id_type=MESH
        )

    started = []

    def go(*args):
        copy = remote(*args)
        copy.start()
        started.append(copy)

    fetches[0].wait()
    fetches[1].wait()
    eight[0:4, :] = inputs_ref[...].astype(F32)
    eight[4:8, :] = grad_ref[...].astype(F32)
    mine[...] = pack(eight[...])
    place = core * 16 + chip
    gathered[place] = mine[...]
    pl.semaphore_wait(barrier, n_chip + len(near_own) + len(near_other) + 1)
    for i, offset in enumerate(chip_offsets):
        go(mine, gathered.at[place], send1.at[i], recv1.at[i], (row, chip_peer(offset) * 2 + core))
    go(mine, gathered.at[place], send_core1.at[n_chip], recv_core1.at[n_chip], partner)
    for offset in (4, 12):
        greet(entered, own_plane(offset))
    for i in reversed(range(n_chip)):
        here = gathered.at[core * 16 + chip_peer(chip_offsets[i], -1)]
        remote(mine, here, send1.at[i], recv1.at[i], partner).wait_recv()
        go(here, here, send_core1.at[i], recv_core1.at[i], partner)
    for i in reversed(range(n_chip)):
        there = gathered.at[(1 - core) * 16 + chip_peer(chip_offsets[i], -1)]
        remote(mine, there, send_core1.at[i], recv_core1.at[i], partner).wait_recv()
    there = gathered.at[(1 - core) * 16 + chip]
    remote(mine, there, send_core1.at[n_chip], recv_core1.at[n_chip], partner).wait_recv()

    groups = unpack(gathered[...])
    for i, value in enumerate(mix(groups[:16], groups[16:])):
        tokens[i] = value.reshape(128, 384).astype(BF16)
    fetches[2].wait()
    fetches[3].wait()

    far_sum, close_sum = far_offsets(near_sum), near_offsets(near_sum)
    n_far_sum = len(far_sum)

    def columns(half, p):
        return pl.ds(pl.multiple_of(half * 384 + cuts[p][0], 128), cuts[p][1])

    def hidden_sums(half, p):
        width = cuts[p][1]
        first = dot(tokens[0], weight_in_ref[:, columns(half, p)], 1, 0).reshape(16, 8, width)
        second = dot(tokens[1], weight_out_ref[columns(half, p), :], 1, 1).reshape(16, 8, width)
        return [value.reshape(8, 16, width) for value in mix(first, second)]

    for p, (sums, own_sums, crossed, passed, parts, hidden) in enumerate(per_cut):
        for i, value in enumerate(hidden_sums(1 - x_hi, p)):
            sums[0, 8 * i : 8 * i + 8] = value.astype(BF16)
        for i, offset in enumerate(far_sum):
            go(sums.at[0, at_z(offset)], crossed.at[i], send_x2.at[p, i], recv_x2.at[p, i], opposite)
        for i, offset in enumerate(close_sum + [0]):
            j = Z - 1 + i
            go(sums.at[0, at_z(offset)], parts.at[j], send2.at[p, j], recv2.at[p, j], other_plane(offset))
    for p, (sums, own_sums, crossed, passed, parts, hidden) in enumerate(per_cut):
        for i, value in enumerate(hidden_sums(x_hi, p)):
            own_sums[8 * i : 8 * i + 8] = value
            sums[1, 8 * i : 8 * i + 8] = value.astype(BF16)
        for i, offset in enumerate(close_sum):
            j = n_far_sum + i
            go(sums.at[1, at_z(offset)], parts.at[j], send2.at[p, j], recv2.at[p, j], own_plane(offset))
    pl.semaphore_wait(entered, 2)
    for p, (sums, own_sums, crossed, passed, parts, hidden) in enumerate(per_cut):
        for i, offset in enumerate(far_sum):
            remote(sums.at[0, z], crossed.at[i], send_x2.at[p, i], recv_x2.at[p, i], opposite).wait_recv()
            passed[i] = (own_sums[at_z(offset)] + crossed[i].astype(F32)).astype(BF16)
            go(passed.at[i], parts.at[i], send2.at[p, i], recv2.at[p, i], own_plane(offset))

    far_send, close_send = far_offsets(near_send), near_offsets(near_send)
    n_far_send = len(far_send)
    for p, (sums, own_sums, crossed, passed, parts, hidden) in enumerate(per_cut):
        width = cuts[p][1]
        total = own_sums[z]
        for j in reversed(range(n_far_sum, Z + len(close_sum))):
            remote(sums.at[0, z], parts.at[j], send2.at[p, j], recv2.at[p, j], opposite).wait_recv()
            total += parts[j].astype(F32)
        for j in reversed(range(n_far_sum)):
            remote(sums.at[0, z], parts.at[j], send2.at[p, j], recv2.at[p, j], opposite).wait_recv()
            total += parts[j].astype(F32)
        total = total.reshape(2, 8, width)
        pre = pltpu.roll(total, 4, 1).astype(BF16).astype(F32)
        own = total.astype(BF16).astype(F32)
        act_row = lax.broadcasted_iota(jnp.int32, total.shape, 1) < 4
        value = jnp.where(act_row, gelu_value(own), total * gelu_slope(pre))
        hidden[x_hi, z] = value.astype(BF16).reshape(16, width)
        block = hidden.at[x_hi, z]
        for i, offset in enumerate(far_send + close_send):
            go(block, block, send3.at[p, i], recv3.at[p, i], own_plane(offset))
        for i, offset in enumerate(close_send + [0]):
            j = Z - 1 + i
            go(block, block, send3.at[p, j], recv3.at[p, j], other_plane(offset))
    for p in range(n_cut):
        hidden = per_cut[p][5]
        for i in reversed(range(n_far_send)):
            here = hidden.at[x_hi, at_z(Z - far_send[i])]
            remote(here, here, send3.at[p, i], recv3.at[p, i], opposite).wait_recv()
            go(here, here, send_x3.at[p, i], recv_x3.at[p, i], opposite)

    def model_sums(half, p):
        width = cuts[p][1]
        value = per_cut[p][5][half].astype(F32).reshape(32, 8, width)
        act, grad_pre = [t.reshape(128, width).astype(BF16) for t in mix(value[:16], value[16:])]
        spread[0, :, columns(half, p)] = act
        spread[1, :, columns(half, p)] = grad_pre
        return dot(act, weight_out_ref[columns(half, p), :], 1, 0), dot(grad_pre, weight_in_ref[:, columns(half, p)], 1, 1)

    first = second = 0.0
    for p in range(n_cut):
        hidden = per_cut[p][5]
        for i, offset in enumerate(close_send):
            here = hidden.at[x_hi, at_z(Z - offset)]
            j = n_far_send + i
            remote(here, here, send3.at[p, j], recv3.at[p, j], opposite).wait_recv()
        more = model_sums(x_hi, p)
        first, second = first + more[0], second + more[1]
    for p in range(n_cut):
        hidden = per_cut[p][5]
        for i, offset in enumerate(close_send + [0]):
            j = Z - 1 + i
            there = hidden.at[1 - x_hi, at_z(Z - offset)]
            remote(there, there, send3.at[p, j], recv3.at[p, j], opposite).wait_recv()
        for i in reversed(range(n_far_send)):
            there = hidden.at[1 - x_hi, at_z(Z - far_send[i])]
            remote(there, there, send_x3.at[p, i], recv_x3.at[p, i], opposite).wait_recv()
        more = model_sums(1 - x_hi, p)
        first, second = first + more[0], second + more[1]
    for i, value in enumerate(mix(first.reshape(16, 8, 384), second.reshape(16, 8, 384))):
        product[i] = value
    go(product.at[1 - core], pair_in, send_core4, recv_core4, partner)
    remote(product.at[0], pair_in, send_core4, recv_core4, partner).wait_recv()
    chip_out[...] = pack(product[core] + pair_in[...])
    for i, offset in enumerate(chip_offsets):
        to = chip_peer(offset)
        go(chip_out.at[to], chip_in.at[i], send4.at[i], recv4.at[i], (row, to * 2 + core))

    grad_weight_out_ref[...] = dot(spread[0], tokens[1], 0, 0).astype(BF16)
    grad_weight_in_ref[...] = dot(tokens[0], spread[1], 0, 0).astype(BF16)
    kept = [
        pltpu.make_async_copy(src, dst, keep.at[i])
        for i, (src, dst) in enumerate((
            (grad_weight_in_ref, grad_weight_in_hbm), (grad_weight_out_ref, grad_weight_out_hbm),
            (out_ref, out_hbm), (grad_inputs_ref, grad_inputs_hbm),
        ))
    ]
    kept[0].start()
    kept[1].start()
    result = product[core, chip] + pair_in[chip]
    for i in reversed(range(n_chip)):
        remote(chip_out.at[chip], chip_in.at[i], send4.at[i], recv4.at[i], partner).wait_recv()
        result += unpack(chip_in[i])
    eight[...] = result
    out_ref[...] = eight[0:4, :].astype(BF16)
    grad_inputs_ref[...] = eight[4:8, :].astype(BF16)
    kept[2].start()
    kept[3].start()
    for copy in started:
        copy.wait_send()
    for copy in kept:
        copy.wait()


def store(*refs):
    sources, targets, held, load, done = refs[:4], refs[4:8], refs[8:12], refs[12], refs[13]
    order = (2, 3, 0, 1)
    loads = [pltpu.make_async_copy(sources[i], held[i], load.at[i]) for i in order]
    copies = [pltpu.make_async_copy(held[i], targets[i], done.at[i]) for i in order]
    for copy in loads:
        copy.start()
    for first, second in zip(loads, copies):
        first.wait()
        second.start()
    for copy in copies:
        copy.wait()


def local(inputs, weight_in, weight_out, grad_out):
    hbm = pl.BlockSpec(memory_space=pltpu.HBM)
    dma = pltpu.SemaphoreType.DMA
    shapes = tuple(
        jax.ShapeDtypeStruct(a.shape, BF16) for a in (inputs, inputs, weight_in, weight_out)
    )
    whole = [pltpu.VMEM(a.shape, BF16) for a in shapes]
    per_cut = []
    for _, width in cuts:
        n_far = len(far_offsets(near_sum))
        per_cut += [
            pltpu.VMEM((2, Z, 16, width), BF16),
            pltpu.VMEM((Z, 16, width), F32),
            pltpu.VMEM((n_far, 16, width), BF16),
            pltpu.VMEM((n_far, 16, width), BF16),
            pltpu.VMEM((n_row, 16, width), BF16),
            pltpu.VMEM((2, Z, 16, width), BF16),
        ]
    far = (n_cut, len(far_offsets(near_sum))), (n_cut, len(far_offsets(near_send)))
    results = pl.pallas_call(
        kernel,
        out_shape=shapes,
        in_specs=[hbm] * 4,
        out_specs=[hbm] * 4,
        scratch_shapes=[
            *whole,
            *[pltpu.VMEM(a.shape, BF16) for a in (inputs, weight_in, weight_out, grad_out)],
            pltpu.VMEM((8, 384), F32),
            pltpu.VMEM((16, 256), BF16),
            pltpu.VMEM((32, 16, 256), BF16),
            pltpu.VMEM((2, 128, 384), BF16),
            pltpu.VMEM((2, 128, 768), BF16),
            pltpu.VMEM((2, 16, 8, 384), F32),
            pltpu.VMEM((16, 8, 384), F32),
            pltpu.VMEM((16, 16, 256), BF16),
            pltpu.VMEM((n_chip, 16, 256), BF16),
            *per_cut,
            dma((4,)), dma((4,)), pltpu.SemaphoreType.REGULAR,
            dma((n_chip,)), dma((n_chip,)), dma((n_chip + 1,)), dma((n_chip + 1,)),
            dma(far[0]), dma(far[0]), dma((n_cut, n_row)), dma((n_cut, n_row)),
            dma((n_cut, n_row)), dma((n_cut, n_row)), dma(far[1]), dma(far[1]),
            dma, dma, dma((n_chip,)), dma((n_chip,)),
        ],
        compiler_params=pltpu.CompilerParams(collective_id=0, has_side_effects=True),
    )(inputs, weight_in, weight_out, grad_out)
    return pl.pallas_call(
        store,
        out_shape=shapes,
        in_specs=[hbm] * 4,
        out_specs=[hbm] * 4,
        scratch_shapes=[*whole, dma((4,)), dma((4,))],
    )(*results)


def solution(mesh):
    placed = (P("col", "row"), P("row", "col"), P("col", "row"), P("col", "row"))
    return jax.shard_map(
        local,
        mesh=mesh,
        in_specs=placed,
        out_specs=(P("col", "row"), P("col", "row"), P("row", "col"), P("col", "row")),
        check_vma=False,
    )
```

time: 87.5 us -> 72.9 us (0.83)
  Pallas kernels: 80.3 us -> 72 us
  local copies, waits for them, and re-layouts: 6.27 us -> 0 us
    pallas_call x1 -> x2, Pallas kernels: 80.3 us -> 72 us  [the longest x1 69.9 us: local(): pl.pallas_call(kernel, out_shape=shapes, in_specs=[hbm] * 4, out_specs=[h...]
    unnamed x12 -> x0, local copies, waits for them, and re-layouts: 6.27 us -> none
where the time goes in v2:
time: 72.9 us; the launch traced here: 72.7 us
  Pallas kernels  72 us (99%)
    pallas_call x1, Pallas kernels, local(): pl.pallas_call(kernel, out_shape=shapes, in_specs=[hbm] * 4, out_specs=[h...  69.9 us
    pallas_call x1, Pallas kernels, local(): pl.pallas_call(store, out_shape=shapes, in_specs=[hbm] * 4, out_specs=[hb...  2.15 us

profile of v2, /device:TPU:1, one launch (start us, length us, event | category | flops | bytes accessed | tf_op | source)
XLA Modules:
  0.0 72.7 jit_solution(7125423645136384825)
XLA Ops:
  0.6 69.9 %shard_map.75 = (bf16[4,384]{1,0:T(4,128)(2,1)}, bf16[4,384]{1,0:T(4,128)(2,1)}, bf16[384,768]{1,0:T(8,128)(2,1)}, bf16[768,384]{1,0:T(8,128)(2,1)}) custom-call(bf16[4,384]{1,0:T(4,128)(2,1)} %inputs_hbm.1, bf16[384,768]{1,0:T(8,128)(2,1)} %weight_in_hbm.1, bf16[768,384]{1,0:T(8,128)(2,1)} %weight_out_hbm.1, bf16[4,384]{1,0:T(4,128)(2,1)} %grad_hbm.1), custom_call_target="tpu_custom_call" | custom-call | tf_op jit(solution)/shard_map/pallas_call | solution.py:330
  70.5 2.1 %shard_map.76 = (bf16[4,384]{1,0:T(4,128)(2,1)}, bf16[4,384]{1,0:T(4,128)(2,1)}, bf16[384,768]{1,0:T(8,128)(2,1)}, bf16[768,384]{1,0:T(8,128)(2,1)}) custom-call(bf16[4,384]{1,0:T(4,128)(2,1)} %get-tuple-element.8.refs_0_, bf16[4,384]{1,0:T(4,128)(2,1)} %get-tuple-element.9.refs_1_, bf16[384,768]{1,0:T(8,128)(2,1)} %get-tuple-element.10.refs_2_, ...), custom_call_target="tpu_custom_call" | custom-call | tf_op jit(solution)/shard_map/pallas_call | solution.py:356

commit v3 on v2

--- a/solution.py
+++ b/solution.py
@@ -13,7 +13,7 @@
 gelu_coef = math.sqrt(2.0 / math.pi)
 Z, Y = 16, 8
 
-cuts = ((0, 256), (256, 128))
+cuts = ((0, 128), (128, 256))
 n_cut = len(cuts)
 
 
@@ -25,7 +25,8 @@
     return [k for d in range(near, 0, -1) for k in (d, Z - d)]
 
 
-near_sum, near_send = 2, 2
+near_sum = 0
+n_first = 4
 chip_offsets = sorted(
     [(h, k) for h in range(2) for k in range(Y) if (h, k) != (0, 0)],
     key=lambda t: -(min(t[1], Y - t[1]) + t[0]),
@@ -110,7 +111,7 @@
     barrier = pltpu.get_barrier_semaphore()
     for offset in chip_offsets:
         greet(barrier, (row, chip_peer(offset) * 2 + core))
-    near_own, near_other = near_offsets(4), near_offsets(max(near_sum, near_send)) + [0]
+    near_own, near_other = near_offsets(4), near_offsets(near_sum) + [0]
     for offset in near_own:
         greet(barrier, own_plane(offset))
     for offset in near_other:
@@ -201,8 +202,12 @@
             passed[i] = (own_sums[at_z(offset)] + crossed[i].astype(F32)).astype(BF16)
             go(passed.at[i], parts.at[i], send2.at[p, i], recv2.at[p, i], own_plane(offset))
 
-    far_send, close_send = far_offsets(near_send), near_offsets(near_send)
-    n_far_send = len(far_send)
+    far_send = far_offsets(0)
+
+    def send_hidden(p, offset):
+        block = per_cut[p][5].at[x_hi, z]
+        remote(block, block, send3.at[p, offset], recv3.at[p, offset], own_plane(offset)).start()
+
     for p, (sums, own_sums, crossed, passed, parts, hidden) in enumerate(per_cut):
         width = cuts[p][1]
         total = own_sums[z]
@@ -219,17 +224,22 @@
         value = jnp.where(act_row, gelu_value(own), total * gelu_slope(pre))
         hidden[x_hi, z] = value.astype(BF16).reshape(16, width)
         block = hidden.at[x_hi, z]
-        for i, offset in enumerate(far_send + close_send):
-            go(block, block, send3.at[p, i], recv3.at[p, i], own_plane(offset))
-        for i, offset in enumerate(close_send + [0]):
-            j = Z - 1 + i
-            go(block, block, send3.at[p, j], recv3.at[p, j], other_plane(offset))
+        for target in range(n_first):
+            @pl.when(z != target)
+            def _():
+                send_hidden(p, (target - z + Z) % Z)
+        go(block, block, send3.at[p, 0], recv3.at[p, 0], opposite)
+    for p in range(n_cut):
+        for offset in far_send:
+            @pl.when(at_z(offset) >= n_first)
+            def _():
+                send_hidden(p, offset)
     for p in range(n_cut):
         hidden = per_cut[p][5]
-        for i in reversed(range(n_far_send)):
-            here = hidden.at[x_hi, at_z(Z - far_send[i])]
-            remote(here, here, send3.at[p, i], recv3.at[p, i], opposite).wait_recv()
-            go(here, here, send_x3.at[p, i], recv_x3.at[p, i], opposite)
+        for offset in reversed(far_send):
+            here = hidden.at[x_hi, at_z(Z - offset)]
+            remote(here, here, send3.at[p, offset], recv3.at[p, offset], opposite).wait_recv()
+            go(here, here, send_x3.at[p, offset], recv_x3.at[p, offset], opposite)
 
     def model_sums(half, p):
         width = cuts[p][1]
@@ -241,22 +251,15 @@
 
     first = second = 0.0
     for p in range(n_cut):
-        hidden = per_cut[p][5]
-        for i, offset in enumerate(close_send):
-            here = hidden.at[x_hi, at_z(Z - offset)]
-            j = n_far_send + i
-            remote(here, here, send3.at[p, j], recv3.at[p, j], opposite).wait_recv()
         more = model_sums(x_hi, p)
         first, second = first + more[0], second + more[1]
     for p in range(n_cut):
         hidden = per_cut[p][5]
-        for i, offset in enumerate(close_send + [0]):
-            j = Z - 1 + i
+        there = hidden.at[1 - x_hi, z]
+        remote(there, there, send3.at[p, 0], recv3.at[p, 0], opposite).wait_recv()
+        for offset in reversed(far_send):
             there = hidden.at[1 - x_hi, at_z(Z - offset)]
-            remote(there, there, send3.at[p, j], recv3.at[p, j], opposite).wait_recv()
-        for i in reversed(range(n_far_send)):
-            there = hidden.at[1 - x_hi, at_z(Z - far_send[i])]
-            remote(there, there, send_x3.at[p, i], recv_x3.at[p, i], opposite).wait_recv()
+            remote(there, there, send_x3.at[p, offset], recv_x3.at[p, offset], opposite).wait_recv()
         more = model_sums(1 - x_hi, p)
         first, second = first + more[0], second + more[1]
     for i, value in enumerate(mix(first.reshape(16, 8, 384), second.reshape(16, 8, 384))):
@@ -290,6 +293,10 @@
     kept[3].start()
     for copy in started:
         copy.wait_send()
+    for p in range(n_cut):
+        for offset in far_send:
+            block = per_cut[p][5].at[x_hi, z]
+            remote(block, block, send3.at[p, offset], recv3.at[p, offset], opposite).wait_send()
     for copy in kept:
         copy.wait()
 
@@ -326,7 +333,7 @@
             pltpu.VMEM((n_row, 16, width), BF16),
             pltpu.VMEM((2, Z, 16, width), BF16),
         ]
-    far = (n_cut, len(far_offsets(near_sum))), (n_cut, len(far_offsets(near_send)))
+    far = n_cut, len(far_offsets(near_sum))
     results = pl.pallas_call(
         kernel,
         out_shape=shapes,
@@ -347,8 +354,8 @@
             *per_cut,
             dma((4,)), dma((4,)), pltpu.SemaphoreType.REGULAR,
             dma((n_chip,)), dma((n_chip,)), dma((n_chip + 1,)), dma((n_chip + 1,)),
-            dma(far[0]), dma(far[0]), dma((n_cut, n_row)), dma((n_cut, n_row)),
-            dma((n_cut, n_row)), dma((n_cut, n_row)), dma(far[1]), dma(far[1]),
+            dma(far), dma(far), dma((n_cut, n_row)), dma((n_cut, n_row)),
+            dma((n_cut, Z)), dma((n_cut, Z)), dma((n_cut, Z)), dma((n_cut, Z)),
             dma, dma, dma((n_chip,)), dma((n_chip,)),
         ],
         compiler_params=pltpu.CompilerParams(collective_id=0, has_side_effects=True),

time: 72.9 us -> 69.4 us (0.952)
  Pallas kernels: 72 us -> 68.6 us
    pallas_call x1, Pallas kernels: 69.9 us -> 66.4 us  [local(): pl.pallas_call(kernel, out_shape=shapes, in_specs=[hbm] * 4, out_specs=[h...]
where the time goes in v3:
time: 69.4 us; the launch traced here: 69.2 us
  Pallas kernels  68.6 us (99%)
    pallas_call x1, Pallas kernels, local(): pl.pallas_call(kernel, out_shape=shapes, in_specs=[hbm] * 4, out_specs=[h...  66.4 us
    pallas_call x1, Pallas kernels, local(): pl.pallas_call(store, out_shape=shapes, in_specs=[hbm] * 4, out_specs=[hb...  2.15 us

profile of v3, /device:TPU:1, one launch (start us, length us, event | category | flops | bytes accessed | tf_op | source)
XLA Modules:
  0.0 69.2 jit_solution(6968390863040302623)
XLA Ops:
  0.6 66.4 %shard_map.75 = (bf16[4,384]{1,0:T(4,128)(2,1)}, bf16[4,384]{1,0:T(4,128)(2,1)}, bf16[384,768]{1,0:T(8,128)(2,1)}, bf16[768,384]{1,0:T(8,128)(2,1)}) custom-call(bf16[4,384]{1,0:T(4,128)(2,1)} %inputs_hbm.1, bf16[384,768]{1,0:T(8,128)(2,1)} %weight_in_hbm.1, bf16[768,384]{1,0:T(8,128)(2,1)} %weight_out_hbm.1, bf16[4,384]{1,0:T(4,128)(2,1)} %grad_hbm.1), custom_call_target="tpu_custom_call" | custom-call | tf_op jit(solution)/shard_map/pallas_call | solution.py:337
  67.1 2.1 %shard_map.76 = (bf16[4,384]{1,0:T(4,128)(2,1)}, bf16[4,384]{1,0:T(4,128)(2,1)}, bf16[384,768]{1,0:T(8,128)(2,1)}, bf16[768,384]{1,0:T(8,128)(2,1)}) custom-call(bf16[4,384]{1,0:T(4,128)(2,1)} %get-tuple-element.8.refs_0_, bf16[4,384]{1,0:T(4,128)(2,1)} %get-tuple-element.9.refs_1_, bf16[384,768]{1,0:T(8,128)(2,1)} %get-tuple-element.10.refs_2_, ...), custom_call_target="tpu_custom_call" | custom-call | tf_op jit(solution)/shard_map/pallas_call | solution.py:363
